TPU v7x, 32 devices: a whole 2x2x4 slice. The times are simulated.
32 devices in a mesh: groups: 2 (over y), wide: 8 (over z, x), narrow: 2 (over core).
Axes of the slice: x: 2, y: 2, z: 4, core: 2. Of those that a mesh axis runs over, the one named last changes fastest.
Arguments:
- pieces: bfloat16 [2, 1024, 8192], P(None, ('groups', 'wide'), 'narrow'), parts along dimension 1, may hold values from -6 to 6
- destination: int32 [512], P('wide'), may hold values from 0 to 511, as said below
- first_offset: int32 [512], P('wide'), may hold values from 0 to 6144, as said below
- valid_length: int32 [512], P('wide'), may hold values from 2048 to 8192
- midpoint_factor: float32 [1024, 128], P(('groups', 'wide')), parts along dimension 0, may hold values from -0.3 to 0.3
- offset_factor: float32 [16384, 128], P(('groups', 'narrow')), parts along dimension 0, may hold values from -6 to 6
- threshold: float32 [16384], P(('groups', 'narrow')), parts along dimension 0, may hold values from 0.3 to 3
Outputs:
- sparse: bfloat16 [2, 1024, 8192], P(None, ('groups', 'wide'), 'narrow'), parts along dimension 1
- new_midpoint: float32 [1024, 128], P(('groups', 'wide')), parts along dimension 0
- new_offset: float32 [16384, 128], P(('groups', 'narrow')), parts along dimension 0
There are 2 independent parts, one for each index of `groups`. A program takes and returns all parts, laid end to end along the dimension named above; an argument that names none is the same for every part. Nothing has to cross between parts.
Inputs may be any that keep to these rules, and one draw needn't show every extreme that they name: destination is a permutation of the midpoint rows; the 64 segments of one device (aligned blocks) name at most 16 rows of any aligned block of 64 midpoint rows, and exactly 16 rows of some block. first_offset + valid_length <= 8192.
All inputs are finite; a program needn't handle non-finite values.
Results may differ from a plain program's by a relative error of at most 0.005.
Values may be sent and summed in bfloat16 or wider, within the bound.
A program may use at most 64 MiB of HBM per device.

v0:
```python
import jax
import jax.numpy as jnp
from jax import lax
from jax.sharding import PartitionSpec as P

ITERS = 2


epsilon = 1e-06


def refine(observed, inside, row_factor, left_factor, right_factor, threshold):
    half_rank = right_factor.shape[1] // 2
    right_low = right_factor.astype(jnp.bfloat16)
    right_turn = jnp.concatenate(
        [-right_factor[:, half_rank:], right_factor[:, :half_rank]], 1
    ).astype(jnp.bfloat16)
    row_turn = jnp.concatenate([row_factor[:, half_rank:], -row_factor[:, :half_rank]], 1)
    model_real = jnp.dot(row_factor, right_low.T, preferred_element_type=jnp.float32)
    model_imag = jnp.dot(row_factor, right_turn.T, preferred_element_type=jnp.float32)
    resid_real = jnp.where(inside, observed[0].astype(jnp.float32) - model_real, jnp.float32(0.0))
    resid_imag = jnp.where(inside, observed[1].astype(jnp.float32) - model_imag, jnp.float32(0.0))
    magnitude = jnp.sqrt(resid_real * resid_real + resid_imag * resid_imag)
    factor = jnp.maximum(magnitude - threshold[None, :], 0.0) / jnp.maximum(
        magnitude, threshold[None, :]
    )
    sparse_real = resid_real * factor
    sparse_imag = resid_imag * factor
    error_real = (resid_real - sparse_real).astype(jnp.bfloat16)
    error_imag = (resid_imag - sparse_imag).astype(jnp.bfloat16)
    row_grad = jnp.dot(error_real, right_low, preferred_element_type=jnp.float32) + jnp.dot(
        error_imag, right_turn, preferred_element_type=jnp.float32
    )
    right_norm = jnp.sum(right_factor[:, :half_rank] ** 2 + right_factor[:, half_rank:] ** 2, 0)
    row_grad, right_norm = lax.psum((row_grad, right_norm), "narrow")
    row_step = row_grad / (jnp.concatenate([right_norm, right_norm]) + epsilon)
    offset_grad = jnp.dot(error_real.T, row_factor, preferred_element_type=jnp.float32) + jnp.dot(
        error_imag.T, row_turn, preferred_element_type=jnp.float32
    )
    left_norm = jnp.sum(left_factor[:, :half_rank] ** 2 + left_factor[:, half_rank:] ** 2, 0)
    offset_grad, left_norm = lax.psum((offset_grad, left_norm), "wide")
    right_next = right_factor + offset_grad / (jnp.concatenate([left_norm, left_norm]) + epsilon)
    return (jnp.stack([sparse_real, sparse_imag]), row_step, right_next)


def local(
    pieces, destination, first_offset, valid_length, midpoint_factor, offset_factor, threshold
):
    row_count = destination.shape[0]
    wide_count = lax.axis_size("wide")
    capacity = 2 * row_count // wide_count
    slot_count = wide_count * capacity
    owner_dev = destination // row_count
    row_in = destination % row_count
    one_hot = (owner_dev[:, None] == jnp.arange(wide_count, dtype=jnp.int32)[None, :]).astype(
        jnp.int32
    )
    before = jnp.cumsum(one_hot, 0) - one_hot
    rank_in = jnp.sum(before * one_hot, 1)
    send_slot = owner_dev * capacity + rank_in
    source_row = (
        jnp.zeros((slot_count,), jnp.int32)
        .at[send_slot]
        .set(jnp.arange(row_count, dtype=jnp.int32))
    )
    filled = jnp.zeros((slot_count,), jnp.bool_).at[send_slot].set(True)
    col_count = pieces.shape[2]
    columns = lax.axis_index("narrow") * col_count + jnp.arange(col_count, dtype=jnp.int32)
    left_factor = midpoint_factor
    right_factor = offset_factor
    request = jnp.where(filled, row_in[source_row], row_count)
    asked_rows = lax.all_to_all(request, "wide", split_axis=0, concat_axis=0, tiled=True)
    asked_valid = asked_rows < row_count
    safe_rows = jnp.minimum(asked_rows, row_count - 1)
    landing = (
        jnp.zeros((row_count,), jnp.int32)
        .at[asked_rows]
        .set(jnp.arange(slot_count, dtype=jnp.int32), mode="drop")
    )
    inside = (columns[None, :] >= first_offset[:, None]) & (
        columns[None, :] < (first_offset + valid_length)[:, None]
    )
    for sweep in range(ITERS):
        answer = jnp.where(
            asked_valid[:, None],
            jnp.take(left_factor.astype(jnp.bfloat16), safe_rows, axis=0),
            jnp.zeros((), jnp.bfloat16),
        )
        fetched = lax.all_to_all(answer, "wide", split_axis=0, concat_axis=0, tiled=True)
        row_factor = jnp.take(fetched, send_slot, axis=0)
        sparse, row_step, right_factor = refine(
            pieces, inside, row_factor, left_factor, right_factor, threshold
        )
        outgoing = jnp.where(
            filled[:, None], jnp.take(row_step, source_row, axis=0), jnp.float32(0.0)
        )
        arriving = lax.all_to_all(
            outgoing.astype(jnp.bfloat16), "wide", split_axis=0, concat_axis=0, tiled=True
        ).astype(outgoing.dtype)
        left_factor = left_factor + jnp.take(arriving, landing, axis=0)
    result = sparse.astype(jnp.bfloat16)
    return (result, left_factor, right_factor)


def solution(mesh):
    placed = (
        P(None, ("groups", "wide"), "narrow"),
        P("wide"),
        P("wide"),
        P("wide"),
        P(("groups", "wide"), None),
        P(("groups", "narrow"), None),
        P(("groups", "narrow")),
    )
    return jax.shard_map(
        local,
        mesh=mesh,
        in_specs=placed,
        out_specs=(
            P(None, ("groups", "wide"), "narrow"),
            P(("groups", "wide"), None),
            P(("groups", "narrow"), None),
        ),
        check_vma=False,
    )
```

profile of v0, /device:TPU:0, one launch (start us, length us, event | category | flops | bytes accessed | tf_op | source)
XLA Modules:
  0.0 268.7 jit_solution(9825216113704867588)
XLA Ops:
  7.2 0.7 and_select_fusion
  8.2 0.8 scatter_custom_fusion.1
  9.0 0.8 scatter_custom_fusion
  9.8 1.2 gather_fusion
  11.1 0.7 all_to_all.36
  11.7 7.3 %all-to-all-start = ((s32[8,16,1]{1,2,0:T(1,128)}), s32[8,16,1]{1,2,0:T(1,128)S(1)}, u32[]{:S(2)}, u32[]{:S(2)}) async-start(s32[8,16,1]{1,2,0:T(1,128)} %bitcast.1), calls=%async_computation | async-start | bytes 8192 | tf_op jit(solution)/shard_map/all_to_all | solution.py:72
  19.0 4.0 %add_reduce_fusion.1 = (f32[64]{0:T(128)S(1)}, bf16[4096,64]{1,0:T(8,128)(2,1)}) fusion(f32[4096,128]{1,0:T(8,128)} %param.20), kind=kLoop, calls=%fused_computation.26 | loop fusion | flops 1572800 | bytes 2621696 | tf_op jit(solution)/shard_map/reduce_sum | solution.py:34
  23.8 1.6 all-to-all-done
  25.9 0.7 fusion.38
  26.8 0.7 gather_fusion.1
  27.5 0.7 select_select_fusion.3
  28.2 4.4 %all-to-all-start.1 = ((bf16[8,16,128]{2,1,0:T(8,128)(2,1)}), bf16[8,16,128]{2,1,0:T(8,128)(2,1)S(1)}, u32[]{:S(2)}, u32[]{:S(2)}) async-start(bf16[8,16,128]{2,1,0:T(8,128)(2,1)} %bitcast.4), calls=%async_computation.1 | async-start | bytes 65536 | tf_op jit(solution)/shard_map/all_to_all | solution.py:89
  32.8 1.0 scatter_custom_fusion.2
  33.8 5.5 %all-to-all-done.1 = bf16[8,16,128]{2,1,0:T(8,128)(2,1)S(1)} async-done(((bf16[8,16,128]{2,1,0:T(8,128)(2,1)}), bf16[8,16,128]{2,1,0:T(8,128)(2,1)S(1)}, u32[]{:S(2)}, u32[]{:S(2)}) %all-to-all-start.1) | async-done | bytes 32800 | tf_op jit(solution)/shard_map/all_to_all | solution.py:89
  39.3 0.6 gather_fusion.2
  40.0 1.7 fusion.3
  41.8 1.5 fusion.5
  44.2 1.8 convolution_add_fusion.1
  46.1 2.1 convolution_add_fusion.3
  48.2 3.5 %all-reduce.2 = (f32[64,128]{1,0:T(8,128)S(1)}, f32[64]{0:T(128)S(1)}) all-reduce(f32[64,128]{1,0:T(8,128)S(1)} %convolution_add_fusion.3, f32[64]{0:T(128)S(1)} %get-tuple-element.27), channel_id=1, replica_groups=mesh['groups'=2,'wide'=8,'narrow'=2] {'narrow'}, use_global_device_ids=true, to_apply=%region_4.7 | all-reduce | flops 8256 | bytes 66048 | tf_op jit(solution)/shard_map/psum | solution.py:35
  51.7 0.7 gather_fusion.3
  52.4 0.7 fusion.15
  53.1 3.3 %all-to-all-start.2 = ((bf16[8,16,128]{2,1,0:T(8,128)(2,1)}), bf16[8,16,128]{2,1,0:T(8,128)(2,1)S(1)}, u32[]{:S(2)}, u32[]{:S(2)}) async-start(bf16[8,16,128]{2,1,0:T(8,128)(2,1)} %bitcast.7), calls=%async_computation.2 | async-start | bytes 65536 | tf_op jit(solution)/shard_map/all_to_all | solution.py:97
  56.5 7.2 %all-to-all-done.2 = bf16[8,16,128]{2,1,0:T(8,128)(2,1)S(1)} async-done(((bf16[8,16,128]{2,1,0:T(8,128)(2,1)}), bf16[8,16,128]{2,1,0:T(8,128)(2,1)S(1)}, u32[]{:S(2)}, u32[]{:S(2)}) %all-to-all-start.2) | async-done | bytes 32800 | tf_op jit(solution)/shard_map/all_to_all | solution.py:97
  64.4 0.7 gather_fusion.5
  65.1 0.7 select_select_fusion.2
  65.8 3.3 %all-to-all-start.3 = ((bf16[8,16,128]{2,1,0:T(8,128)(2,1)}), bf16[8,16,128]{2,1,0:T(8,128)(2,1)S(1)}, u32[]{:S(2)}, u32[]{:S(2)}) async-start(bf16[8,16,128]{2,1,0:T(8,128)(2,1)} %bitcast.9), calls=%async_computation.3 | async-start | bytes 65536 | tf_op jit(solution)/shard_map/all_to_all | solution.py:89
  69.3 22.0 %all-reduce = (f32[64]{0:T(128)S(1)}, f32[64]{0:T(128)S(1)}) all-reduce(f32[64]{0:T(128)S(1)} %get-tuple-element.36, f32[64]{0:T(128)S(1)} %get-tuple-element.35), channel_id=1, replica_groups=mesh['groups'=2,'wide'=8,'narrow'=2] {'wide'}, use_global_device_ids=true, to_apply=%region_10.15 | all-reduce | flops 128 | bytes 1024 | tf_op jit(solution)/shard_map/psum | solution.py:41
  91.4 0.6 gather_fusion.6
  92.2 54.5 %all-reduce.6.cloned.1.call-done = f32[4096,128]{1,0:T(8,128)} async-done(((f32[4096,128]{1,0:T(8,128)}), f32[4096,128]{1,0:T(8,128)}) %all-reduce.6.cloned.1.call-update) | async-done | bytes 2097168 | tf_op jit(solution)/shard_map/psum | solution.py:41
  146.7 1.8 divide_add_fusion.1
  148.7 0.6 add_reduce_fusion
  149.3 1.4 copy-done.11
  150.7 0.8 fusion
  151.5 2.2 subtract_convert_fusion
  154.7 1.8 convolution_add_fusion
  156.6 1.5 copy-done.2
  158.1 1.3 fusion.8
  159.4 0.7 convolution_add_fusion.2
  160.1 3.5 %all-reduce.1 = (f32[64,128]{1,0:T(8,128)S(1)}, f32[64]{0:T(128)S(1)}) all-reduce(f32[64,128]{1,0:T(8,128)S(1)} %convolution_add_fusion.2, f32[64]{0:T(128)S(1)} %get-tuple-element.25), channel_id=1, replica_groups=mesh['groups'=2,'wide'=8,'narrow'=2] {'narrow'}, use_global_device_ids=true, to_apply=%region_11.16 | all-reduce | flops 8256 | bytes 66048 | tf_op jit(solution)/shard_map/psum | solution.py:35
  163.7 0.7 gather_fusion.7
  164.4 0.7 fusion.14
  165.1 4.3 %all-to-all-start.4 = ((bf16[8,16,128]{2,1,0:T(8,128)(2,1)}), bf16[8,16,128]{2,1,0:T(8,128)(2,1)S(1)}, u32[]{:S(2)}, u32[]{:S(2)}) async-start(bf16[8,16,128]{2,1,0:T(8,128)(2,1)} %bitcast.14), calls=%async_computation.4 | async-start | bytes 65536 | tf_op jit(solution)/shard_map/all_to_all | solution.py:97
  169.5 2.3 pad_maximum_fusion.2
  171.8 4.9 %all-to-all-done.4 = bf16[8,16,128]{2,1,0:T(8,128)(2,1)S(1)} async-done(((bf16[8,16,128]{2,1,0:T(8,128)(2,1)}), bf16[8,16,128]{2,1,0:T(8,128)(2,1)S(1)}, u32[]{:S(2)}, u32[]{:S(2)}) %all-to-all-start.4) | async-done | bytes 32800 | tf_op jit(solution)/shard_map/all_to_all | solution.py:97
  177.2 0.7 select_add_fusion
  177.9 80.9 %all-reduce.8.cloned.1.call-done = f32[4096,128]{1,0:T(8,128)} async-done(((f32[4096,128]{1,0:T(8,128)}), f32[4096,128]{1,0:T(8,128)}) %all-reduce.8.cloned.1.call-update) | async-done | bytes 2097168 | tf_op jit(solution)/shard_map/psum | solution.py:41
  258.8 3.1 %divide_add_fusion = f32[4096,128]{1,0:T(8,128)} fusion(f32[4096,128]{1,0:T(8,128)S(1)} %copy-done.2, f32[4096,128]{1,0:T(8,128)} %all-reduce.8.cloned.1.call-done, f32[128]{0:T(128)S(1)} %maximum_add_fusion.3), kind=kLoop, calls=%fused_computation.22 | loop fusion | flops 1048576 | bytes 6291968 | tf_op jit(solution)/shard_map/add | solution.py:42
  (83 shorter events, 6.1 us)
Async XLA Ops:
  11.7 13.6 %all-to-all-start = ((s32[8,16,1]{1,2,0:T(1,128)}), s32[8,16,1]{1,2,0:T(1,128)S(1)}, u32[]{:S(2)}, u32[]{:S(2)}) async-start(s32[8,16,1]{1,2,0:T(1,128)} %bitcast.1), calls=%async_computation | async-start | bytes 8192 | tf_op jit(solution)/shard_map/all_to_all | solution.py:72
  19.0 4.0 %copy-start = (f32[4096,128]{1,0:T(8,128)S(1)}, f32[4096,128]{1,0:T(8,128)}, u32[]{:S(2)}) copy-start(f32[4096,128]{1,0:T(8,128)} %param.20) | copy-start | bytes 6291460
  23.0 0.8 copy-start.12
  23.0 0.8 copy-start.13
  23.0 0.8 copy-start.15
  26.8 15.0 %copy-start.14 = (f32[4096]{0:T(1024)S(1)}, f32[4096]{0:T(1024)}, u32[]{:S(2)}) copy-start(f32[4096]{0:T(1024)} %param.21) | copy-start | bytes 49156
  28.2 11.1 %all-to-all-start.1 = ((bf16[8,16,128]{2,1,0:T(8,128)(2,1)}), bf16[8,16,128]{2,1,0:T(8,128)(2,1)S(1)}, u32[]{:S(2)}, u32[]{:S(2)}) async-start(bf16[8,16,128]{2,1,0:T(8,128)(2,1)} %bitcast.4), calls=%async_computation.1 | async-start | bytes 65536 | tf_op jit(solution)/shard_map/all_to_all | solution.py:89
  32.6 114.1 %all-reduce.6.cloned.1.call-start = ((), (), s32[]{:S(2)}) async-start(), calls=%async_computation.5 | async-start | bytes 4194304 | tf_op jit(solution)/shard_map/psum | solution.py:41
  40.0 1.8 copy-start.5
  40.0 1.8 copy-start.10
  43.3 0.9 copy-start.9
  53.1 10.5 %all-to-all-start.2 = ((bf16[8,16,128]{2,1,0:T(8,128)(2,1)}), bf16[8,16,128]{2,1,0:T(8,128)(2,1)S(1)}, u32[]{:S(2)}, u32[]{:S(2)}) async-start(bf16[8,16,128]{2,1,0:T(8,128)(2,1)} %bitcast.7), calls=%async_computation.2 | async-start | bytes 65536 | tf_op jit(solution)/shard_map/all_to_all | solution.py:97
  65.8 25.6 %all-to-all-start.3 = ((bf16[8,16,128]{2,1,0:T(8,128)(2,1)}), bf16[8,16,128]{2,1,0:T(8,128)(2,1)S(1)}, u32[]{:S(2)}, u32[]{:S(2)}) async-start(bf16[8,16,128]{2,1,0:T(8,128)(2,1)} %bitcast.9), calls=%async_computation.3 | async-start | bytes 65536 | tf_op jit(solution)/shard_map/all_to_all | solution.py:89
  69.1 189.6 %all-reduce.8.cloned.1.call-start = ((), (), s32[]{:S(2)}) async-start(), calls=%async_computation.6 | async-start | bytes 4194304 | tf_op jit(solution)/shard_map/psum | solution.py:41
  148.5 3.0 %copy-start.1 = (f32[4096,128]{1,0:T(8,128)}, f32[4096,128]{1,0:T(8,128)S(1)}, u32[]{:S(2)}) copy-start(f32[4096,128]{1,0:T(8,128)S(1)} %divide_add_fusion.1) | copy-start | bytes 6291460
  148.6 2.0 copy-start.11
  149.3 4.4 %copy-start.3 = (bf16[4096,64]{1,0:T(8,128)(2,1)}, bf16[4096,64]{1,0:T(8,128)(2,1)S(1)}, u32[]{:S(2)}) copy-start(bf16[4096,64]{1,0:T(8,128)(2,1)S(1)} %get-tuple-element.26) | copy-start | bytes 1572868
  153.7 0.8 copy-start.6
  153.7 1.0 copy-start.8
  156.5 1.6 copy-start.2
  156.5 2.9 %copy-start.4 = (bf16[4096,64]{1,0:T(8,128)(2,1)S(1)}, bf16[4096,64]{1,0:T(8,128)(2,1)}, u32[]{:S(2)}) copy-start(bf16[4096,64]{1,0:T(8,128)(2,1)} %copy-done.3) | copy-start | bytes 1572868
  156.5 2.9 %copy-start.7 = (bf16[64,4096]{1,0:T(8,128)(2,1)S(1)}, bf16[64,4096]{1,0:T(8,128)(2,1)}, u32[]{:S(2)}) copy-start(bf16[64,4096]{1,0:T(8,128)(2,1)} %copy-done.6) | copy-start | bytes 1572868
  165.1 11.5 %all-to-all-start.4 = ((bf16[8,16,128]{2,1,0:T(8,128)(2,1)}), bf16[8,16,128]{2,1,0:T(8,128)(2,1)S(1)}, u32[]{:S(2)}, u32[]{:S(2)}) async-start(bf16[8,16,128]{2,1,0:T(8,128)(2,1)} %bitcast.14), calls=%async_computation.4 | async-start | bytes 65536 | tf_op jit(solution)/shard_map/all_to_all | solution.py:97
Sparse Core Ops, SparseCore 0:
  46.2 100.4 all-reduce.5
  156.6 102.0 all-reduce.7
where the time goes:
time: 270 us; the launch traced here: 269 us
  waiting for transfers between devices  155 us (57%)
  blocking collectives  28.9 us (11%)
  starting transfers between devices  22.8 us (8%)
  other arithmetic  18 us (7%)
  matrix products  15.3 us (6%)
  local copies, waits for them, and re-layouts  14.8 us (5%)
  between operations  14.4 us (5%)
    psum x2, waiting for transfers between devices, refine(): offset_grad, left_norm = lax.psum((offset_grad, left_norm), 'wide')  135 us
    psum x1, blocking collectives, refine(): offset_grad, left_norm = lax.psum((offset_grad, left_norm), 'wide')  22 us
    all_to_all x2, waiting for transfers between devices, local(): lax.all_to_all(outgoing.astype(jnp.bfloat16), 'wide', split_axis=0, conca...  12 us
    all_to_all x2, starting transfers between devices, local(): lax.all_to_all(answer, 'wide', split_axis=0, concat_axis=0, tiled=True)  7.74 us
    all_to_all x2, starting transfers between devices, local(): lax.all_to_all(outgoing.astype(jnp.bfloat16), 'wide', split_axis=0, conca...  7.69 us
    all_to_all x1, starting transfers between devices, local(): lax.all_to_all(request, 'wide', split_axis=0, concat_axis=0, tiled=True)  7.25 us
    psum x2, blocking collectives, refine(): row_grad, right_norm = lax.psum((row_grad, right_norm), 'narrow')  6.91 us
    all_to_all x2, waiting for transfers between devices, local(): lax.all_to_all(answer, 'wide', split_axis=0, concat_axis=0, tiled=True)  5.54 us
  transfers between devices with their start and end apart: 7, of which 6 were waited for; matrix products, arithmetic and copies ran while one was open for 7% of the time, Pallas kernels for 0%

commit v1 on v0

v1 whole, which is shorter than its diff:
```python
import functools

import jax
import jax.numpy as jnp
from jax import lax
from jax.experimental import pallas as pl
from jax.experimental.pallas import tpu as pltpu
from jax.sharding import PartitionSpec as P

ITERS = 2
CHUNKS = 8

epsilon = 1e-06
F32 = jnp.float32
BF16 = jnp.bfloat16
MESH = pl.DeviceIdType.MESH


def swap_halves(x):
    half = x.shape[1] // 2
    return jnp.concatenate([x[:, half:], x[:, :half]], 1)


def turned(x):
    half = x.shape[1] // 2
    return jnp.concatenate([x[:, half:], -x[:, :half]], 1)


def kernel(
    wide,
    chunk,
    pieces,
    dest,
    first,
    valid,
    u_in,
    v_in,
    thr,
    sp_out,
    u_out,
    v_out,
    v_low,
    acc,
    sent,
    got,
    total,
    stack,
    u_seg,
    row_acc,
    u_high,
    u_rest,
    own_high,
    own_rest,
    norm_own,
    norms,
    row_own,
    row_peer,
    step_own,
    steps,
    rs_send,
    rs_recv,
    ag_send,
    ag_recv,
    high_send,
    high_recv,
    rest_send,
    rest_recv,
    norm_send,
    norm_recv,
    row_send,
    row_recv,
    step_send,
    step_recv,
):
    g = lax.axis_index("groups")
    w = lax.axis_index("wide")
    n = lax.axis_index("narrow")
    rows, rank2 = u_in.shape
    cols = v_in.shape[0]
    chunks = cols // chunk
    bits = wide.bit_length() - 1
    peers = [lax.bitwise_xor(w, jnp.int32(j)) for j in range(1, wide)]
    side = 1 - n
    pending = []

    def send(src, dst, s_sem, r_sem, to_wide=None, to_narrow=None):
        copy = pltpu.make_async_remote_copy(
            src_ref=src,
            dst_ref=dst,
            send_sem=s_sem,
            recv_sem=r_sem,
            device_id=(g, w if to_wide is None else to_wide, n if to_narrow is None else to_narrow),
            device_id_type=MESH,
        )
        copy.start()
        pending.append(copy)
        return copy

    barrier = pltpu.get_barrier_semaphore()
    for p in peers:
        pl.semaphore_signal(barrier, inc=1, device_id=(g, p, n), device_id_type=MESH)
    pl.semaphore_signal(barrier, inc=1, device_id=(g, w, side), device_id_type=MESH)

    u0 = u_in[...]
    high = u0.astype(BF16)
    own_high[...] = high
    own_rest[...] = (u0 - high.astype(F32)).astype(BF16)
    u_high[w] = own_high[...]
    u_rest[w] = own_rest[...]
    part = jnp.broadcast_to(jnp.sum(u0 * u0, 0, keepdims=True), (8, rank2))
    norm_own[0] = part
    norms[0, w] = part
    pl.semaphore_wait(barrier, wide)

    waits = {}

    def gather(name, src, dst, s_sem, r_sem):
        for j, p in enumerate(peers):
            waits.setdefault(name, []).append(
                send(src, dst, s_sem.at[j], r_sem.at[j], to_wide=p)
            )

    def finish(name):
        for copy in waits[name]:
            copy.wait_recv()

    gather("high", own_high, u_high.at[w], high_send, high_recv)
    gather("norm0", norm_own.at[0], norms.at[0, w], norm_send.at[0], norm_recv.at[0])
    gather("rest", own_rest, u_rest.at[w], rest_send, rest_recv)

    eye = lax.broadcasted_iota(jnp.int32, (rows, rows), 0) == lax.broadcasted_iota(
        jnp.int32, (rows, rows), 1
    )

    def column(ref):
        wide_row = jnp.broadcast_to(ref[...].astype(F32), (rows, rows))
        return jnp.sum(jnp.where(eye, wide_row, 0.0), 1, keepdims=True).astype(jnp.int32)

    dest_col = column(dest)
    begin_col = column(first) - n * cols
    end_col = begin_col + column(valid)
    pick = (
        lax.broadcasted_iota(jnp.int32, (rows, wide * rows), 1) == dest_col
    ).astype(BF16)

    square = jnp.zeros((1, rank2), F32)
    for c in range(chunks):
        at = pl.ds(c * chunk, chunk)
        v = v_in[at]
        v_low[at] = v.astype(BF16)
        square = square + jnp.sum(v * v, 0, keepdims=True)
    squares = [square, jnp.zeros((1, rank2), F32)]

    def left_ready(value):
        low = value.astype(BF16)
        stack[:rows] = low
        stack[rows:] = turned(low.astype(F32)).astype(BF16)

    finish("high")
    picked_high = jnp.dot(
        pick, u_high[...].reshape(wide * rows, rank2), preferred_element_type=F32
    )
    left_ready(picked_high)

    def left_scale(it):
        finish("norm%d" % it)
        s = norms[it, 0, :1]
        for j in range(1, wide):
            s = s + norms[it, j, :1]
        return 1.0 / (s + swap_halves(s) + epsilon)

    scale = [None] * ITERS
    flights = {}

    def order(c):
        base = list(range(bits))
        if c % 2 and bits > 1:
            base[0], base[1] = base[1], base[0]
        return base

    def bit_of(b):
        return lax.bitwise_and(lax.shift_right_logical(w, jnp.int32(b)), 1)

    def place(c, s):
        start, size = jnp.int32(c * chunk), chunk
        for b in order(c)[:s]:
            size //= 2
            start = start + bit_of(b) * size
        return pl.multiple_of(start, size), size

    def scatter_send(it, c, s):
        b = order(c)[s]
        start, size = place(c, s)
        half = size // 2
        away = pl.ds(pl.multiple_of(start + (1 - bit_of(b)) * half, half), half)
        sent[it, away] = acc[away].astype(BF16)
        slot = chunk - size
        flights[it, c, s] = send(
            sent.at[it, away],
            got.at[it, c, pl.ds(slot, half)],
            rs_send.at[it, c, s],
            rs_recv.at[it, c, s],
            to_wide=lax.bitwise_xor(w, jnp.int32(1 << b)),
        )

    def scatter_take(it, c, s):
        flights[it, c, s].wait_recv()
        start, size = place(c, s + 1)
        mine = pl.ds(start, size)
        summed = acc[mine] + got[it, c, pl.ds(chunk - 2 * size, size)].astype(F32)
        if s == bits - 1:
            total[it, mine] = summed.astype(BF16)
        else:
            acc[mine] = summed

    def gather_send(it, c, s):
        start, size = place(c, s + 1)
        mine = pl.ds(start, size)
        flights[it, c, "g", s] = send(
            total.at[it, mine],
            total.at[it, mine],
            ag_send.at[it, c, s],
            ag_recv.at[it, c, s],
            to_wide=lax.bitwise_xor(w, jnp.int32(1 << order(c)[s])),
        )

    def compute(it, c):
        at = pl.ds(c * chunk, chunk)
        low = v_low[at]
        left = stack[...]
        model = lax.dot_general(left, low, (((1,), (1,)), ((), ())), preferred_element_type=F32)
        lane = lax.broadcasted_iota(jnp.int32, (rows, chunk), 1) + c * chunk
        inside = (lane >= begin_col) & (lane < end_col)
        real = jnp.where(inside, pieces[0, :, at].astype(F32) - model[:rows], 0.0)
        imag = jnp.where(inside, pieces[1, :, at].astype(F32) - model[rows:], 0.0)
        keep = jnp.minimum(thr[:, at] * lax.rsqrt(real * real + imag * imag), 1.0)
        err_real = real * keep
        err_imag = imag * keep
        if it == ITERS - 1:
            sp_out[0, :, at] = (real - err_real).astype(BF16)
            sp_out[1, :, at] = (imag - err_imag).astype(BF16)
        err = jnp.concatenate([err_real, err_imag], 0).astype(BF16)
        row = jnp.dot(err, low, preferred_element_type=F32)
        row_acc[...] = row if c == 0 else row_acc[...] + row
        acc[at] = lax.dot_general(err, left, (((0,), (0,)), ((), ())), preferred_element_type=F32)
        scatter_send(it, c, 0)

    def row_exchange(it):
        row = row_acc[...]
        row_own[it, :rows] = row[:rows] - turned(row[rows:])
        row_own[it, rows:] = jnp.broadcast_to(squares[it], (8, rank2))
        flights[it, "row"] = send(
            row_own.at[it], row_peer.at[it], row_send.at[it], row_recv.at[it], to_narrow=side
        )

    def row_step(it):
        flights[it, "row"].wait_recv()
        both = row_own[it] + row_peer[it]
        square = both[rows : rows + 1]
        return both[:rows] / (square + swap_halves(square) + epsilon)

    def update(it, c):
        at = pl.ds(c * chunk, chunk)
        if scale[it] is None:
            scale[it] = left_scale(it)
        source = v_in if it == 0 else v_out
        new = source[at] + total[it, at].astype(F32) * scale[it]
        v_out[at] = new
        if it < ITERS - 1:
            v_low[at] = new.astype(BF16)
            squares[it + 1] = squares[it + 1] + jnp.sum(new * new, 0, keepdims=True)

    def stage(it, c, s):
        if s == 0:
            compute(it, c)
        elif s <= bits:
            scatter_take(it, c, s - 1)
            if s < bits:
                scatter_send(it, c, s)
            else:
                gather_send(it, c, bits - 1)
        else:
            r = 2 * bits - s
            flights[it, c, "g", r].wait_recv()
            if r > 0:
                gather_send(it, c, r - 1)
            else:
                update(it, c)

    last = 2 * bits
    spacing = max(chunks, last)
    step_sum = None
    for t in range(spacing * (ITERS - 1) + chunks + last):
        for it in range(ITERS):
            local_t = t - it * spacing
            if it > 0 and local_t == 0:
                step = row_step(it - 1)
                if it == 1:
                    finish("rest")
                    u_seg[...] = picked_high + jnp.dot(
                        pick,
                        u_rest[...].reshape(wide * rows, rank2),
                        preferred_element_type=F32,
                    )
                step_sum = step if step_sum is None else step_sum + step
                value = u_seg[...] + step
                u_seg[...] = value
                left_ready(value)
                part = jnp.broadcast_to(jnp.sum(value * value, 0, keepdims=True), (8, rank2))
                norm_own[it] = part
                norms[it, w] = part
                gather(
                    "norm%d" % it,
                    norm_own.at[it],
                    norms.at[it, w],
                    norm_send.at[it],
                    norm_recv.at[it],
                )
            for s in range(last, -1, -1):
                c = local_t - s
                if 0 <= c < chunks:
                    stage(it, c, s)
                    if s == 0 and c == chunks - 1:
                        row_exchange(it)
        if t == spacing * (ITERS - 1) + chunks:
            step_sum = step_sum + row_step(ITERS - 1)
            spread = (
                lax.broadcasted_iota(jnp.int32, (wide * rows, rows), 0)
                == jnp.broadcast_to(dest[...], (wide * rows, rows))
            ).astype(BF16)
            placed = jnp.dot(spread, step_sum.astype(BF16), preferred_element_type=F32)
            step_own[...] = placed.astype(BF16).reshape(wide, rows, rank2)
            steps[w] = step_own[w]
            for j, p in enumerate(peers):
                waits.setdefault("step", []).append(
                    send(
                        step_own.at[p], steps.at[w], step_send.at[j], step_recv.at[j], to_wide=p
                    )
                )
    finish("step")
    out = u_in[...]
    for j in range(wide):
        out = out + steps[j].astype(F32)
    u_out[...] = out
    for copy in pending:
        copy.wait_send()


def local(
    pieces, destination, first_offset, valid_length, midpoint_factor, offset_factor, threshold
):
    wide = lax.axis_size("wide")
    rows, rank2 = midpoint_factor.shape
    cols = offset_factor.shape[0]
    chunk = max(cols // CHUNKS, 16 * wide)
    chunks = cols // chunk
    bits = wide.bit_length() - 1
    vmem = pl.BlockSpec(memory_space=pltpu.VMEM)
    dma = pltpu.SemaphoreType.DMA
    return pl.pallas_call(
        functools.partial(kernel, wide, chunk),
        out_shape=(
            jax.ShapeDtypeStruct(pieces.shape, BF16),
            jax.ShapeDtypeStruct(midpoint_factor.shape, F32),
            jax.ShapeDtypeStruct(offset_factor.shape, F32),
        ),
        in_specs=[vmem] * 7,
        out_specs=(vmem,) * 3,
        scratch_shapes=[
            pltpu.VMEM((cols, rank2), BF16),
            pltpu.VMEM((cols, rank2), F32),
            pltpu.VMEM((ITERS, cols, rank2), BF16),
            pltpu.VMEM((ITERS, chunks, chunk, rank2), BF16),
            pltpu.VMEM((ITERS, cols, rank2), BF16),
            pltpu.VMEM((2 * rows, rank2), BF16),
            pltpu.VMEM((rows, rank2), F32),
            pltpu.VMEM((2 * rows, rank2), F32),
            pltpu.VMEM((wide, rows, rank2), BF16),
            pltpu.VMEM((wide, rows, rank2), BF16),
            pltpu.VMEM((rows, rank2), BF16),
            pltpu.VMEM((rows, rank2), BF16),
            pltpu.VMEM((ITERS, 8, rank2), F32),
            pltpu.VMEM((ITERS, wide, 8, rank2), F32),
            pltpu.VMEM((ITERS, rows + 8, rank2), F32),
            pltpu.VMEM((ITERS, rows + 8, rank2), F32),
            pltpu.VMEM((wide, rows, rank2), BF16),
            pltpu.VMEM((wide, rows, rank2), BF16),
            dma((ITERS, chunks, bits)),
            dma((ITERS, chunks, bits)),
            dma((ITERS, chunks, bits)),
            dma((ITERS, chunks, bits)),
            dma((wide - 1,)),
            dma((wide - 1,)),
            dma((wide - 1,)),
            dma((wide - 1,)),
            dma((ITERS, wide - 1)),
            dma((ITERS, wide - 1)),
            dma((ITERS,)),
            dma((ITERS,)),
            dma((wide - 1,)),
            dma((wide - 1,)),
        ],
        compiler_params=pltpu.CompilerParams(
            collective_id=0, has_side_effects=True, vmem_limit_bytes=48 * 1024 * 1024
        ),
        cost_estimate=pl.CostEstimate(
            flops=ITERS * 3 * 4 * rows * rank2 * cols,
            bytes_accessed=12 * cols * rank2,
            transcendentals=0,
        ),
    )(
        pieces,
        destination.reshape(1, rows),
        first_offset.reshape(1, rows),
        valid_length.reshape(1, rows),
        midpoint_factor,
        offset_factor,
        threshold.reshape(1, cols),
    )


def solution(mesh):
    placed = (
        P(None, ("groups", "wide"), "narrow"),
        P("wide"),
        P("wide"),
        P("wide"),
        P(("groups", "wide"), None),
        P(("groups", "narrow"), None),
        P(("groups", "narrow")),
    )
    return jax.shard_map(
        local,
        mesh=mesh,
        in_specs=placed,
        out_specs=(
            P(None, ("groups", "wide"), "narrow"),
            P(("groups", "wide"), None),
            P(("groups", "narrow"), None),
        ),
        check_vma=False,
    )
```

time: 270 us -> 111 us (0.41)
  waiting for transfers between devices: 155 us -> 0 us
  Pallas kernels: 0 us -> 103 us
  blocking collectives: 28.9 us -> 0 us
  starting transfers between devices: 22.8 us -> 0 us
  other arithmetic: 18 us -> 0 us
  matrix products: 15.3 us -> 0 us
  between operations: 14.4 us -> 0.66 us
  local copies, waits for them, and re-layouts: 14.8 us -> 7.56 us
    psum x2 -> x0, waiting for transfers between devices: 135 us -> none  [refine(): offset_grad, left_norm = lax.psum((offset_grad, left_norm), 'wide')]
    pallas_call x0 -> x1, Pallas kernels: none -> 103 us  [local(): pl.pallas_call(functools.partial(kernel, wide, chunk), out_shape=(jax.Sha...]
    psum x3 -> x0, blocking collectives: 28.9 us -> none  [the longest x1 22 us: refine(): offset_grad, left_norm = lax.psum((offset_grad, left_norm), 'wide')]
    all_to_all x5 -> x0, starting transfers between devices: 22.7 us -> none  [the longest x2 7.74 us: local(): lax.all_to_all(answer, 'wide', split_axis=0, concat_axis=0, tiled=True)]
    all_to_all x5 -> x0, waiting for transfers between devices: 19.2 us -> none  [the longest x2 12 us: local(): lax.all_to_all(outgoing.astype(jnp.bfloat16), 'wide', split_axis=0, conca...]
    dot_general x12 -> x0, matrix products: 15.3 us -> none  [the longest x2 3.87 us: refine(): jnp.dot(row_factor, right_low.T, preferred_element_type=jnp.float32)]
    gather x9 -> x0, local copies, waits for them, and re-layouts: 6.55 us -> none  [the longest x2 1.43 us: local(): jnp.take(left_factor.astype(jnp.bfloat16), safe_rows, axis=0)]
    add x9 -> x0, other arithmetic: 5.92 us -> none  [the longest x2 4.91 us: refine(): right_factor + offset_grad / (jnp.concatenate([left_norm, left_norm]) + e...]
  transfers between devices with their start and end apart: 7 -> 0, of which waited for: 6 -> 0; matrix products, arithmetic and copies ran while one was open for 7% -> 0% of each run, Pallas kernels for 0% -> 0%
where the time goes in v1:
time: 111 us
  Pallas kernels  103 us (93%)
  local copies, waits for them, and re-layouts  7.56 us (7%)
    pallas_call x1, Pallas kernels, local(): pl.pallas_call(functools.partial(kernel, wide, chunk), out_shape=(jax.Sha...  103 us
    unnamed x15, local copies, waits for them, and re-layouts  7.56 us

profile of v1, /device:TPU:0, one launch (start us, length us, event | category | flops | bytes accessed | tf_op | source)
XLA Modules:
  0.0 111.0 jit_solution(6914394262618427884)
XLA Ops:
  0.6 0.0 copy-start
  0.6 1.2 %copy-done = bf16[2,64,4096]{2,1,0:T(8,128)(2,1)S(1)} copy-done((bf16[2,64,4096]{2,1,0:T(8,128)(2,1)S(1)}, bf16[2,64,4096]{2,1,0:T(8,128)(2,1)}, u32[]{:S(2)}) %copy-start) | copy-done | bytes 1048600
  1.9 0.0 copy-start.1
  1.9 0.8 copy-done.1
  2.6 0.0 copy-start.2
  2.6 0.7 copy-done.2
  3.3 0.0 copy-start.3
  3.3 0.7 copy-done.3
  4.0 0.0 copy-start.4
  4.0 0.7 copy-done.4
  4.6 0.0 copy-start.5
  4.6 0.7 copy-done.5
  5.3 102.8 %shard_map.94 = (bf16[2,64,4096]{2,1,0:T(8,128)(2,1)S(1)}, f32[64,128]{1,0:T(8,128)S(1)}, f32[4096,128]{1,0:T(8,128)S(1)}) custom-call(bf16[2,64,4096]{2,1,0:T(8,128)(2,1)S(1)} %copy-done, s32[1,64]{1,0:T(1,128)S(1)} %bitcast.5, s32[1,64]{1,0:T(1,128)S(1)} %bitcast.6, s32[1,64]{1,0:T(1,128)S(1)} %bitcast.7, f32[64,128]{1,0:T(8,128)S(1)} %copy-done.1, ...), custom_call_target="tpu_custom_call" | custom-call | flops 805306368 | bytes 6291456 | tf_op jit(solution)/shard_map/pallas_call | solution.py:360
  108.1 1.0 copy.13
  109.1 0.6 copy.14
  109.7 1.3 %copy.15 = f32[4096,128]{1,0:T(8,128)} copy(f32[4096,128]{1,0:T(8,128)S(1)} %get-tuple-element.8) | data formatting | bytes 4194304
Async XLA Ops:
  0.6 1.2 %copy-start = (bf16[2,64,4096]{2,1,0:T(8,128)(2,1)S(1)}, bf16[2,64,4096]{2,1,0:T(8,128)(2,1)}, u32[]{:S(2)}) copy-start(bf16[2,64,4096]{2,1,0:T(8,128)(2,1)} %pieces.1) | copy-start | bytes 3145732
  1.9 0.8 copy-start.1
  2.6 0.7 copy-start.2
  3.3 0.7 copy-start.3
  4.0 0.7 copy-start.4
  4.6 0.7 copy-start.5

commit v2 on v1

--- a/solution.py
+++ b/solution.py
@@ -9,6 +9,7 @@
 
 ITERS = 2
 CHUNKS = 8
+GAP = 3
 
 epsilon = 1e-06
 F32 = jnp.float32
@@ -29,16 +30,25 @@
 def kernel(
     wide,
     chunk,
+    pieces_hbm,
+    dest_hbm,
+    first_hbm,
+    valid_hbm,
+    u_hbm,
+    v_hbm,
+    thr_hbm,
+    sp_hbm,
+    u_out,
+    v_out_hbm,
     pieces,
     dest,
     first,
     valid,
     u_in,
-    v_in,
+    v_now,
     thr,
-    sp_out,
-    u_out,
-    v_out,
+    in_sem,
+    out_sem,
     v_low,
     acc,
     sent,
@@ -76,12 +86,34 @@
     w = lax.axis_index("wide")
     n = lax.axis_index("narrow")
     rows, rank2 = u_in.shape
-    cols = v_in.shape[0]
+    cols = v_now.shape[0]
     chunks = cols // chunk
     bits = wide.bit_length() - 1
     peers = [lax.bitwise_xor(w, jnp.int32(j)) for j in range(1, wide)]
     side = 1 - n
     pending = []
+    loads = [
+        pltpu.make_async_copy(src, dst, in_sem.at[i])
+        for i, (src, dst) in enumerate(
+            [
+                (u_hbm, u_in),
+                (dest_hbm, dest),
+                (first_hbm, first),
+                (valid_hbm, valid),
+                (v_hbm, v_now),
+                (thr_hbm, thr),
+                (pieces_hbm, pieces),
+            ]
+        )
+    ]
+    for load in loads:
+        load.start()
+    stores = []
+
+    def store(src, dst, sem):
+        copy = pltpu.make_async_copy(src, dst, sem)
+        copy.start()
+        stores.append(copy)
 
     def send(src, dst, s_sem, r_sem, to_wide=None, to_narrow=None):
         copy = pltpu.make_async_remote_copy(
@@ -101,6 +133,7 @@
         pl.semaphore_signal(barrier, inc=1, device_id=(g, p, n), device_id_type=MESH)
     pl.semaphore_signal(barrier, inc=1, device_id=(g, w, side), device_id_type=MESH)
 
+    loads[0].wait()
     u0 = u_in[...]
     high = u0.astype(BF16)
     own_high[...] = high
@@ -126,8 +159,9 @@
 
     gather("high", own_high, u_high.at[w], high_send, high_recv)
     gather("norm0", norm_own.at[0], norms.at[0, w], norm_send.at[0], norm_recv.at[0])
-    gather("rest", own_rest, u_rest.at[w], rest_send, rest_recv)
-
+
+    for load in loads[1:5]:
+        load.wait()
     eye = lax.broadcasted_iota(jnp.int32, (rows, rows), 0) == lax.broadcasted_iota(
         jnp.int32, (rows, rows), 1
     )
@@ -146,7 +180,7 @@
     square = jnp.zeros((1, rank2), F32)
     for c in range(chunks):
         at = pl.ds(c * chunk, chunk)
-        v = v_in[at]
+        v = v_now[at]
         v_low[at] = v.astype(BF16)
         square = square + jnp.sum(v * v, 0, keepdims=True)
     squares = [square, jnp.zeros((1, rank2), F32)]
@@ -156,6 +190,8 @@
         stack[:rows] = low
         stack[rows:] = turned(low.astype(F32)).astype(BF16)
 
+    for load in loads[5:]:
+        load.wait()
     finish("high")
     picked_high = jnp.dot(
         pick, u_high[...].reshape(wide * rows, rank2), preferred_element_type=F32
@@ -237,8 +273,9 @@
         err_real = real * keep
         err_imag = imag * keep
         if it == ITERS - 1:
-            sp_out[0, :, at] = (real - err_real).astype(BF16)
-            sp_out[1, :, at] = (imag - err_imag).astype(BF16)
+            pieces[0, :, at] = (real - err_real).astype(BF16)
+            pieces[1, :, at] = (imag - err_imag).astype(BF16)
+            store(pieces.at[:, :, at], sp_hbm.at[:, :, at], out_sem.at[0, c])
         err = jnp.concatenate([err_real, err_imag], 0).astype(BF16)
         row = jnp.dot(err, low, preferred_element_type=F32)
         row_acc[...] = row if c == 0 else row_acc[...] + row
@@ -263,12 +300,13 @@
         at = pl.ds(c * chunk, chunk)
         if scale[it] is None:
             scale[it] = left_scale(it)
-        source = v_in if it == 0 else v_out
-        new = source[at] + total[it, at].astype(F32) * scale[it]
-        v_out[at] = new
+        new = v_now[at] + total[it, at].astype(F32) * scale[it]
+        v_now[at] = new
         if it < ITERS - 1:
             v_low[at] = new.astype(BF16)
             squares[it + 1] = squares[it + 1] + jnp.sum(new * new, 0, keepdims=True)
+        else:
+            store(v_now.at[at], v_out_hbm.at[at], out_sem.at[1, c])
 
     def stage(it, c, s):
         if s == 0:
@@ -287,56 +325,60 @@
             else:
                 update(it, c)
 
+    def left_update(it):
+        step = row_step(it - 1)
+        if it == 1:
+            finish("rest")
+            u_seg[...] = picked_high + jnp.dot(
+                pick, u_rest[...].reshape(wide * rows, rank2), preferred_element_type=F32
+            )
+        value = u_seg[...] + step
+        u_seg[...] = value
+        left_ready(value)
+        part = jnp.broadcast_to(jnp.sum(value * value, 0, keepdims=True), (8, rank2))
+        norm_own[it] = part
+        norms[it, w] = part
+        gather(
+            "norm%d" % it, norm_own.at[it], norms.at[it, w], norm_send.at[it], norm_recv.at[it]
+        )
+        return step
+
+    def step_exchange(step_sum):
+        spread = (
+            lax.broadcasted_iota(jnp.int32, (wide * rows, rows), 0)
+            == jnp.broadcast_to(dest[...], (wide * rows, rows))
+        ).astype(BF16)
+        placed = jnp.dot(spread, step_sum.astype(BF16), preferred_element_type=F32)
+        step_own[...] = placed.astype(BF16).reshape(wide, rows, rank2)
+        steps[w] = step_own[w]
+        for j, p in enumerate(peers):
+            waits.setdefault("step", []).append(
+                send(step_own.at[p], steps.at[w], step_send.at[j], step_recv.at[j], to_wide=p)
+            )
+
     last = 2 * bits
-    spacing = max(chunks, last)
+    spacing = max(chunks, GAP * last)
+    events = []
+    for it in range(ITERS):
+        for c in range(chunks):
+            for s in range(last + 1):
+                events.append((it * spacing + c + GAP * s, it, -s, "stage", c))
+        events.append((it * spacing + chunks - 1, it, 1, "exchange", 0))
+        events.append((min(it * spacing + chunks - 1 + GAP, (it + 1) * spacing), it, 2, "step", 0))
+    events.append((1, 0, 3, "rest", 0))
     step_sum = None
-    for t in range(spacing * (ITERS - 1) + chunks + last):
-        for it in range(ITERS):
-            local_t = t - it * spacing
-            if it > 0 and local_t == 0:
-                step = row_step(it - 1)
-                if it == 1:
-                    finish("rest")
-                    u_seg[...] = picked_high + jnp.dot(
-                        pick,
-                        u_rest[...].reshape(wide * rows, rank2),
-                        preferred_element_type=F32,
-                    )
-                step_sum = step if step_sum is None else step_sum + step
-                value = u_seg[...] + step
-                u_seg[...] = value
-                left_ready(value)
-                part = jnp.broadcast_to(jnp.sum(value * value, 0, keepdims=True), (8, rank2))
-                norm_own[it] = part
-                norms[it, w] = part
-                gather(
-                    "norm%d" % it,
-                    norm_own.at[it],
-                    norms.at[it, w],
-                    norm_send.at[it],
-                    norm_recv.at[it],
-                )
-            for s in range(last, -1, -1):
-                c = local_t - s
-                if 0 <= c < chunks:
-                    stage(it, c, s)
-                    if s == 0 and c == chunks - 1:
-                        row_exchange(it)
-        if t == spacing * (ITERS - 1) + chunks:
-            step_sum = step_sum + row_step(ITERS - 1)
-            spread = (
-                lax.broadcasted_iota(jnp.int32, (wide * rows, rows), 0)
-                == jnp.broadcast_to(dest[...], (wide * rows, rows))
-            ).astype(BF16)
-            placed = jnp.dot(spread, step_sum.astype(BF16), preferred_element_type=F32)
-            step_own[...] = placed.astype(BF16).reshape(wide, rows, rank2)
-            steps[w] = step_own[w]
-            for j, p in enumerate(peers):
-                waits.setdefault("step", []).append(
-                    send(
-                        step_own.at[p], steps.at[w], step_send.at[j], step_recv.at[j], to_wide=p
-                    )
-                )
+    for _, it, s, what, c in sorted(events):
+        if what == "stage":
+            stage(it, c, -s)
+        elif what == "exchange":
+            row_exchange(it)
+        elif what == "rest":
+            gather("rest", own_rest, u_rest.at[w], rest_send, rest_recv)
+        else:
+            step = left_update(it + 1) if it + 1 < ITERS else row_step(it)
+            step_sum = step if step_sum is None else step_sum + step
+            if it + 1 == ITERS:
+                step_exchange(step_sum)
     finish("step")
     out = u_in[...]
     for j in range(wide):
@@ -344,6 +386,8 @@
     u_out[...] = out
     for copy in pending:
         copy.wait_send()
+    for copy in stores:
+        copy.wait()
 
 
 def local(
@@ -356,6 +400,7 @@
     chunks = cols // chunk
     bits = wide.bit_length() - 1
     vmem = pl.BlockSpec(memory_space=pltpu.VMEM)
+    hbm = pl.BlockSpec(memory_space=pl.ANY)
     dma = pltpu.SemaphoreType.DMA
     return pl.pallas_call(
         functools.partial(kernel, wide, chunk),
@@ -364,9 +409,18 @@
             jax.ShapeDtypeStruct(midpoint_factor.shape, F32),
             jax.ShapeDtypeStruct(offset_factor.shape, F32),
         ),
-        in_specs=[vmem] * 7,
-        out_specs=(vmem,) * 3,
+        in_specs=[hbm] * 7,
+        out_specs=(hbm, vmem, hbm),
         scratch_shapes=[
+            pltpu.VMEM(pieces.shape, BF16),
+            pltpu.VMEM((1, rows), jnp.int32),
+            pltpu.VMEM((1, rows), jnp.int32),
+            pltpu.VMEM((1, rows), jnp.int32),
+            pltpu.VMEM((rows, rank2), F32),
+            pltpu.VMEM((cols, rank2), F32),
+            pltpu.VMEM((1, cols), F32),
+            dma((7,)),
+            dma((2, chunks)),
             pltpu.VMEM((cols, rank2), BF16),
             pltpu.VMEM((cols, rank2), F32),
             pltpu.VMEM((ITERS, cols, rank2), BF16),
@@ -401,7 +455,7 @@
             dma((wide - 1,)),
         ],
         compiler_params=pltpu.CompilerParams(
-            collective_id=0, has_side_effects=True, vmem_limit_bytes=48 * 1024 * 1024
+            collective_id=0, has_side_effects=True, vmem_limit_bytes=56 * 1024 * 1024
         ),
         cost_estimate=pl.CostEstimate(
             flops=ITERS * 3 * 4 * rows * rank2 * cols,

time: 111 us -> 81.1 us (0.73)
  Pallas kernels: 103 us -> 75.1 us
  local copies, waits for them, and re-layouts: 7.56 us -> 5.13 us
    pallas_call x1, Pallas kernels: 103 us -> 75.1 us  [local(): pl.pallas_call(functools.partial(kernel, wide, chunk), out_shape=(jax.Sha...]
    unnamed x15 -> x5, local copies, waits for them, and re-layouts: 7.56 us -> 5.13 us
where the time goes in v2:
time: 81.1 us; the launch traced here: 80.9 us
  Pallas kernels  75.1 us (93%)
  local copies, waits for them, and re-layouts  5.13 us (6%)
    pallas_call x1, Pallas kernels, local(): pl.pallas_call(functools.partial(kernel, wide, chunk), out_shape=(jax.Sha...  75.1 us
    unnamed x5, local copies, waits for them, and re-layouts  5.13 us

profile of v2, /device:TPU:0, one launch (start us, length us, event | category | flops | bytes accessed | tf_op | source)
XLA Modules:
  0.0 80.9 jit_solution(7579033984269881634)
XLA Ops:
  0.6 75.1 %shard_map.94 = (bf16[2,64,4096]{2,1,0:T(8,128)(2,1)}, f32[64,128]{1,0:T(8,128)}, f32[4096,128]{1,0:T(8,128)}) custom-call(bf16[2,64,4096]{2,1,0:T(8,128)(2,1)} %pieces_hbm.1, s32[1,64]{1,0:T(1,128)} %bitcast.5, s32[1,64]{1,0:T(1,128)} %bitcast.6, s32[1,64]{1,0:T(1,128)} %bitcast.7, f32[64,128]{1,0:T(8,128)} %u_hbm.1, f32[4096,128]{1,0:T(8,128)} %v_hbm.1, ...), custom_call_target="tpu_custom_call" | custom-call | flops 805306368 | bytes 6291456 | tf_op jit(solution)/shard_map/pallas_call | solution.py:405
  75.8 0.0 copy-start
  75.8 2.4 %copy.13 = bf16[2,64,4096]{2,1,0:T(8,128)(2,1)} copy(bf16[2,64,4096]{2,1,0:T(8,128)(2,1)} %get-tuple-element.6) | data formatting | bytes 2097152
  78.2 1.4 %copy.14 = f32[64,128]{1,0:T(8,128)} copy(f32[64,128]{1,0:T(8,128)} %get-tuple-element.7) | data formatting | bytes 65536
  79.6 0.0 copy-done
  79.6 1.3 %copy.15 = f32[4096,128]{1,0:T(8,128)} copy(f32[4096,128]{1,0:T(8,128)S(1)} %copy-done) | data formatting | bytes 4194304
Async XLA Ops:
  75.8 3.8 %copy-start = (f32[4096,128]{1,0:T(8,128)S(1)}, f32[4096,128]{1,0:T(8,128)}, u32[]{:S(2)}) copy-start(f32[4096,128]{1,0:T(8,128)} %get-tuple-element.8) | copy-start | bytes 6291460

commit v3 on v2

--- a/solution.py
+++ b/solution.py
@@ -8,13 +8,60 @@
 from jax.sharding import PartitionSpec as P
 
 ITERS = 2
-CHUNKS = 8
-GAP = 3
+CHUNKS = 16
 
 epsilon = 1e-06
 F32 = jnp.float32
 BF16 = jnp.bfloat16
 MESH = pl.DeviceIdType.MESH
+
+
+def order_of(c, bits):
+    base = list(range(bits))
+    if c % 2 and bits > 1:
+        base[0], base[1] = base[1], base[0]
+    return base
+
+
+def plan(chunks, chunk, bits):
+    delay, rate, work, step = 2.0, 45e3, 1.1 * chunk / 512, 0.1
+    last = 2 * bits
+    now, busy, arrived, order = 0.0, [0.0] * bits, {}, []
+    stage_at = {(it, c): 0 for it in range(ITERS) for c in range(chunks)}
+    computed, row_sent, row_done = [0] * ITERS, [None] * ITERS, [False] * ITERS
+    while True:
+        ready = []
+        for (it, c), s in stage_at.items():
+            if s == 0:
+                allowed = it == 0 or (row_done[it - 1] and stage_at[it - 1, c] > last)
+                if c == computed[it] and allowed:
+                    ready.append((now, it, c, s))
+            elif s <= last:
+                ready.append((arrived[it, c], it, c, s))
+        for it in range(ITERS):
+            if row_sent[it] is not None and not row_done[it]:
+                ready.append((row_sent[it] + delay, it, -1, 0))
+        if not ready:
+            return order
+        when, it, c, s = min(ready)
+        now = max(now, when)
+        order.append((it, c, s))
+        if c < 0:
+            row_done[it] = True
+            now += 0.5
+            continue
+        now += work if s == 0 else step + 0.2 * chunk / 512
+        if s == 0:
+            computed[it] += 1
+            if computed[it] == chunks:
+                row_sent[it] = now
+        if s < last:
+            r = s if s < bits else last - 1 - s
+            b = order_of(c, bits)[r]
+            start = max(busy[b], now)
+            busy[b] = start + (chunk * 256 >> (r + 1)) / (rate if b < 2 else rate / 2)
+            arrived[it, c] = busy[b] + delay
+        stage_at[it, c] += 1
 
 
 def swap_halves(x):
@@ -208,24 +255,18 @@
     scale = [None] * ITERS
     flights = {}
 
-    def order(c):
-        base = list(range(bits))
-        if c % 2 and bits > 1:
-            base[0], base[1] = base[1], base[0]
-        return base
-
     def bit_of(b):
         return lax.bitwise_and(lax.shift_right_logical(w, jnp.int32(b)), 1)
 
     def place(c, s):
         start, size = jnp.int32(c * chunk), chunk
-        for b in order(c)[:s]:
+        for b in order_of(c, bits)[:s]:
             size //= 2
             start = start + bit_of(b) * size
         return pl.multiple_of(start, size), size
 
     def scatter_send(it, c, s):
-        b = order(c)[s]
+        b = order_of(c, bits)[s]
         start, size = place(c, s)
         half = size // 2
         away = pl.ds(pl.multiple_of(start + (1 - bit_of(b)) * half, half), half)
@@ -257,7 +298,7 @@
             total.at[it, mine],
             ag_send.at[it, c, s],
             ag_recv.at[it, c, s],
-            to_wide=lax.bitwise_xor(w, jnp.int32(1 << order(c)[s])),
+            to_wide=lax.bitwise_xor(w, jnp.int32(1 << order_of(c, bits)[s])),
         )
 
     def compute(it, c):
@@ -357,23 +398,14 @@
             )
 
     last = 2 * bits
-    spacing = max(chunks, GAP * last)
-    events = []
-    for it in range(ITERS):
-        for c in range(chunks):
-            for s in range(last + 1):
-                events.append((it * spacing + c + GAP * s, it, -s, "stage", c))
-        events.append((it * spacing + chunks - 1, it, 1, "exchange", 0))
-        events.append((min(it * spacing + chunks - 1 + GAP, (it + 1) * spacing), it, 2, "step", 0))
-    events.append((1, 0, 3, "rest", 0))
     step_sum = None
-    for _, it, s, what, c in sorted(events):
-        if what == "stage":
-            stage(it, c, -s)
-        elif what == "exchange":
-            row_exchange(it)
-        elif what == "rest":
+    for index, (it, c, s) in enumerate(plan(chunks, chunk, bits)):
+        if index == min(2, chunks - 1):
             gather("rest", own_rest, u_rest.at[w], rest_send, rest_recv)
+        if c >= 0:
+            stage(it, c, s)
+            if s == 0 and c == chunks - 1:
+                row_exchange(it)
         else:
             step = left_update(it + 1) if it + 1 < ITERS else row_step(it)
             step_sum = step if step_sum is None else step_sum + step
@@ -390,6 +422,26 @@
         copy.wait()
 
 
+PARTS = 4
+
+
+def flush(a, b, c, a_out, b_out, c_out, sem):
+    copies = [pltpu.make_async_copy(b, b_out, sem.at[2 * PARTS])]
+    rows = c.shape[0] // PARTS
+    cols = a.shape[2] // PARTS
+    for i in range(PARTS):
+        at = pl.ds(i * rows, rows)
+        copies.append(pltpu.make_async_copy(c.at[at], c_out.at[at], sem.at[i]))
+        at = pl.ds(i * cols, cols)
+        copies.append(
+            pltpu.make_async_copy(a.at[:, :, at], a_out.at[:, :, at], sem.at[PARTS + i])
+        )
+    for copy in copies:
+        copy.start()
+    for copy in copies:
+        copy.wait()
+
+
 def local(
     pieces, destination, first_offset, valid_length, midpoint_factor, offset_factor, threshold
 ):
@@ -400,9 +452,9 @@
     chunks = cols // chunk
     bits = wide.bit_length() - 1
     vmem = pl.BlockSpec(memory_space=pltpu.VMEM)
-    hbm = pl.BlockSpec(memory_space=pl.ANY)
+    hbm = pl.BlockSpec(memory_space=pltpu.HBM)
     dma = pltpu.SemaphoreType.DMA
-    return pl.pallas_call(
+    results = pl.pallas_call(
         functools.partial(kernel, wide, chunk),
         out_shape=(
             jax.ShapeDtypeStruct(pieces.shape, BF16),
@@ -471,6 +523,14 @@
         offset_factor,
         threshold.reshape(1, cols),
     )
+    return pl.pallas_call(
+        flush,
+        out_shape=tuple(jax.ShapeDtypeStruct(r.shape, r.dtype) for r in results),
+        in_specs=[hbm] * 3,
+        out_specs=(hbm,) * 3,
+        scratch_shapes=[dma((2 * PARTS + 1,))],
+        compiler_params=pltpu.CompilerParams(vmem_limit_bytes=56 * 1024 * 1024),
+    )(*results)
 
 
 def solution(mesh):

time: 81.1 us -> 186 us (2.29)
  Pallas kernels: 75.1 us -> 185 us
  local copies, waits for them, and re-layouts: 5.13 us -> 0 us
    pallas_call x0 -> x1, Pallas kernels: none -> 97.5 us  [local(): pl.pallas_call(flush, out_shape=tuple((jax.ShapeDtypeStruct(r.shape, r.dt...]
    pallas_call x1, Pallas kernels: 75.1 us -> 87.6 us  [local(): pl.pallas_call(functools.partial(kernel, wide, chunk), out_shape=(jax.Sha...]
    unnamed x5 -> x0, local copies, waits for them, and re-layouts: 5.13 us -> none
where the time goes in v3:
time: 186 us
  Pallas kernels  185 us (99%)
    pallas_call x1, Pallas kernels, local(): pl.pallas_call(flush, out_shape=tuple((jax.ShapeDtypeStruct(r.shape, r.dt...  97.5 us
    pallas_call x1, Pallas kernels, local(): pl.pallas_call(functools.partial(kernel, wide, chunk), out_shape=(jax.Sha...  87.6 us

profile of v3, /device:TPU:0, one launch (start us, length us, event | category | flops | bytes accessed | tf_op | source)
XLA Modules:
  0.0 185.7 jit_solution(11797457798150004238)
XLA Ops:
  0.6 87.6 %shard_map.94 = (bf16[2,64,4096]{2,1,0:T(8,128)(2,1)}, f32[64,128]{1,0:T(8,128)}, f32[4096,128]{1,0:T(8,128)}) custom-call(bf16[2,64,4096]{2,1,0:T(8,128)(2,1)} %pieces_hbm.1, s32[1,64]{1,0:T(1,128)} %bitcast.5, s32[1,64]{1,0:T(1,128)} %bitcast.6, s32[1,64]{1,0:T(1,128)} %bitcast.7, f32[64,128]{1,0:T(8,128)} %u_hbm.1, f32[4096,128]{1,0:T(8,128)} %v_hbm.1, ...), custom_call_target="tpu_custom_call" | custom-call | flops 805306368 | bytes 6291456 | tf_op jit(solution)/shard_map/pallas_call | solution.py:457
  88.2 97.5 %shard_map.95 = (bf16[2,64,4096]{2,1,0:T(8,128)(2,1)}, f32[64,128]{1,0:T(8,128)}, f32[4096,128]{1,0:T(8,128)}) custom-call(bf16[2,64,4096]{2,1,0:T(8,128)(2,1)} %get-tuple-element.6.a, f32[64,128]{1,0:T(8,128)} %get-tuple-element.7.b, f32[4096,128]{1,0:T(8,128)} %get-tuple-element.8.c), custom_call_target="tpu_custom_call" | custom-call | tf_op jit(solution)/shard_map/pallas_call | solution.py:526

commit v4 on v3

--- a/solution.py
+++ b/solution.py
@@ -8,7 +8,7 @@
 from jax.sharding import PartitionSpec as P
 
 ITERS = 2
-CHUNKS = 16
+CHUNKS = 8
 
 epsilon = 1e-06
 F32 = jnp.float32
@@ -24,7 +24,7 @@
 
 
 def plan(chunks, chunk, bits):
-    delay, rate, work, step = 2.0, 45e3, 1.1 * chunk / 512, 0.1
+    delay, rate, work, step = 1.6, 45e3, 0.6 + 0.8 * chunk / 512, 0.15
     last = 2 * bits
     now, busy, arrived, order = 0.0, [0.0] * bits, {}, []
     stage_at = {(it, c): 0 for it in range(ITERS) for c in range(chunks)}
@@ -425,21 +425,29 @@
 PARTS = 4
 
 
-def flush(a, b, c, a_out, b_out, c_out, sem):
-    copies = [pltpu.make_async_copy(b, b_out, sem.at[2 * PARTS])]
+def flush(a, b, c, a_out, b_out, c_out, a_held, b_held, c_held, in_sem, out_sem):
     rows = c.shape[0] // PARTS
     cols = a.shape[2] // PARTS
+    moves = []
     for i in range(PARTS):
         at = pl.ds(i * rows, rows)
-        copies.append(pltpu.make_async_copy(c.at[at], c_out.at[at], sem.at[i]))
+        moves.append((c.at[at], c_held.at[at], c_out.at[at]))
         at = pl.ds(i * cols, cols)
-        copies.append(
-            pltpu.make_async_copy(a.at[:, :, at], a_out.at[:, :, at], sem.at[PARTS + i])
-        )
-    for copy in copies:
-        copy.start()
-    for copy in copies:
-        copy.wait()
+        moves.append((a.at[:, :, at], a_held.at[:, :, at], a_out.at[:, :, at]))
+    moves.append((b, b_held, b_out))
+    loads = [
+        pltpu.make_async_copy(src, held, in_sem.at[i]) for i, (src, held, _) in enumerate(moves)
+    ]
+    stores = [
+        pltpu.make_async_copy(held, dst, out_sem.at[i]) for i, (_, held, dst) in enumerate(moves)
+    ]
+    for load in loads:
+        load.start()
+    for load, store in zip(loads, stores):
+        load.wait()
+        store.start()
+    for store in stores:
+        store.wait()
 
 
 def local(
@@ -528,7 +536,8 @@
         out_shape=tuple(jax.ShapeDtypeStruct(r.shape, r.dtype) for r in results),
         in_specs=[hbm] * 3,
         out_specs=(hbm,) * 3,
-        scratch_shapes=[dma((2 * PARTS + 1,))],
+        scratch_shapes=[pltpu.VMEM(r.shape, r.dtype) for r in results]
+        + [dma((2 * PARTS + 1,)), dma((2 * PARTS + 1,))],
         compiler_params=pltpu.CompilerParams(vmem_limit_bytes=56 * 1024 * 1024),
     )(*results)
 

time: 186 us -> 83.8 us (0.45)
  Pallas kernels: 185 us -> 83 us
    pallas_call x1, Pallas kernels: 97.5 us -> 2.85 us  [local(): pl.pallas_call(flush, out_shape=tuple((jax.ShapeDtypeStruct(r.shape, r.dt...]
    pallas_call x1, Pallas kernels: 87.6 us -> 80.1 us  [local(): pl.pallas_call(functools.partial(kernel, wide, chunk), out_shape=(jax.Sha...]
where the time goes in v4:
time: 83.8 us; the launch traced here: 83.6 us
  Pallas kernels  83 us (99%)
    pallas_call x1, Pallas kernels, local(): pl.pallas_call(functools.partial(kernel, wide, chunk), out_shape=(jax.Sha...  80.1 us
    pallas_call x1, Pallas kernels, local(): pl.pallas_call(flush, out_shape=tuple((jax.ShapeDtypeStruct(r.shape, r.dt...  2.85 us

profile of v4, /device:TPU:0, one launch (start us, length us, event | category | flops | bytes accessed | tf_op | source)
XLA Modules:
  0.0 83.6 jit_solution(6728798169303130959)
XLA Ops:
  0.6 80.1 %shard_map.94 = (bf16[2,64,4096]{2,1,0:T(8,128)(2,1)}, f32[64,128]{1,0:T(8,128)}, f32[4096,128]{1,0:T(8,128)}) custom-call(bf16[2,64,4096]{2,1,0:T(8,128)(2,1)} %pieces_hbm.1, s32[1,64]{1,0:T(1,128)} %bitcast.5, s32[1,64]{1,0:T(1,128)} %bitcast.6, s32[1,64]{1,0:T(1,128)} %bitcast.7, f32[64,128]{1,0:T(8,128)} %u_hbm.1, f32[4096,128]{1,0:T(8,128)} %v_hbm.1, ...), custom_call_target="tpu_custom_call" | custom-call | flops 805306368 | bytes 6291456 | tf_op jit(solution)/shard_map/pallas_call | solution.py:465
  80.8 2.9 %shard_map.95 = (bf16[2,64,4096]{2,1,0:T(8,128)(2,1)}, f32[64,128]{1,0:T(8,128)}, f32[4096,128]{1,0:T(8,128)}) custom-call(bf16[2,64,4096]{2,1,0:T(8,128)(2,1)} %get-tuple-element.6.a, f32[64,128]{1,0:T(8,128)} %get-tuple-element.7.b, f32[4096,128]{1,0:T(8,128)} %get-tuple-element.8.c), custom_call_target="tpu_custom_call" | custom-call | tf_op jit(solution)/shard_map/pallas_call | solution.py:534

commit v5 on v4

--- a/solution.py
+++ b/solution.py
@@ -23,45 +23,19 @@
     return base
 
 
-def plan(chunks, chunk, bits):
-    delay, rate, work, step = 1.6, 45e3, 0.6 + 0.8 * chunk / 512, 0.15
+def plan(chunks, bits):
     last = 2 * bits
-    now, busy, arrived, order = 0.0, [0.0] * bits, {}, []
-    stage_at = {(it, c): 0 for it in range(ITERS) for c in range(chunks)}
-    computed, row_sent, row_done = [0] * ITERS, [None] * ITERS, [False] * ITERS
-    while True:
-        ready = []
-        for (it, c), s in stage_at.items():
-            if s == 0:
-                allowed = it == 0 or (row_done[it - 1] and stage_at[it - 1, c] > last)
-                if c == computed[it] and allowed:
-                    ready.append((now, it, c, s))
-            elif s <= last:
-                ready.append((arrived[it, c], it, c, s))
-        for it in range(ITERS):
-            if row_sent[it] is not None and not row_done[it]:
-                ready.append((row_sent[it] + delay, it, -1, 0))
-        if not ready:
-            return order
-        when, it, c, s = min(ready)
-        now = max(now, when)
-        order.append((it, c, s))
-        if c < 0:
-            row_done[it] = True
-            now += 0.5
-            continue
-        now += work if s == 0 else step + 0.2 * chunk / 512
-        if s == 0:
-            computed[it] += 1
-            if computed[it] == chunks:
-                row_sent[it] = now
-        if s < last:
-            r = s if s < bits else last - 1 - s
-            b = order_of(c, bits)[r]
-            start = max(busy[b], now)
-            busy[b] = start + (chunk * 256 >> (r + 1)) / (rate if b < 2 else rate / 2)
-            arrived[it, c] = busy[b] + delay
-        stage_at[it, c] += 1
+    lag = [0]
+    for s in range(last):
+        lag.append(lag[-1] + max(2, 4 - min(s, last - 1 - s)))
+    spacing = max(chunks, lag[last])
+    events = []
+    for it in range(ITERS):
+        for c in range(chunks):
+            for s in range(last + 1):
+                events.append((it * spacing + c + lag[s], it, -s, c))
+        events.append((min(it * spacing + chunks + 2, (it + 1) * spacing), it, 1, -1))
+    return [(it, c, -s) for _, it, s, c in sorted(events)]
 
 
 def swap_halves(x):
@@ -399,7 +373,7 @@
 
     last = 2 * bits
     step_sum = None
-    for index, (it, c, s) in enumerate(plan(chunks, chunk, bits)):
+    for index, (it, c, s) in enumerate(plan(chunks, bits)):
         if index == min(2, chunks - 1):
             gather("rest", own_rest, u_rest.at[w], rest_send, rest_recv)
         if c >= 0:

time: 83.8 us -> 81.3 us (0.970)
  Pallas kernels: 83 us -> 80.5 us
    pallas_call x1, Pallas kernels: 80.1 us -> 77.7 us  [local(): pl.pallas_call(functools.partial(kernel, wide, chunk), out_shape=(jax.Sha...]
where the time goes in v5:
time: 81.3 us; the launch traced here: 81.2 us
  Pallas kernels  80.5 us (99%)
    pallas_call x1, Pallas kernels, local(): pl.pallas_call(functools.partial(kernel, wide, chunk), out_shape=(jax.Sha...  77.7 us
    pallas_call x1, Pallas kernels, local(): pl.pallas_call(flush, out_shape=tuple((jax.ShapeDtypeStruct(r.shape, r.dt...  2.85 us

profile of v5, /device:TPU:0, one launch (start us, length us, event | category | flops | bytes accessed | tf_op | source)
XLA Modules:
  0.0 81.2 jit_solution(5948156397448355506)
XLA Ops:
  0.6 77.7 %shard_map.94 = (bf16[2,64,4096]{2,1,0:T(8,128)(2,1)}, f32[64,128]{1,0:T(8,128)}, f32[4096,128]{1,0:T(8,128)}) custom-call(bf16[2,64,4096]{2,1,0:T(8,128)(2,1)} %pieces_hbm.1, s32[1,64]{1,0:T(1,128)} %bitcast.5, s32[1,64]{1,0:T(1,128)} %bitcast.6, s32[1,64]{1,0:T(1,128)} %bitcast.7, f32[64,128]{1,0:T(8,128)} %u_hbm.1, f32[4096,128]{1,0:T(8,128)} %v_hbm.1, ...), custom_call_target="tpu_custom_call" | custom-call | flops 805306368 | bytes 6291456 | tf_op jit(solution)/shard_map/pallas_call | solution.py:439
  78.3 2.9 %shard_map.95 = (bf16[2,64,4096]{2,1,0:T(8,128)(2,1)}, f32[64,128]{1,0:T(8,128)}, f32[4096,128]{1,0:T(8,128)}) custom-call(bf16[2,64,4096]{2,1,0:T(8,128)(2,1)} %get-tuple-element.6.a, f32[64,128]{1,0:T(8,128)} %get-tuple-element.7.b, f32[4096,128]{1,0:T(8,128)} %get-tuple-element.8.c), custom_call_target="tpu_custom_call" | custom-call | tf_op jit(solution)/shard_map/pallas_call | solution.py:508
